TPU v7x, 512 devices: a whole 4x8x8 slice. The times are simulated.
512 devices in a mesh: gx: 32 (over y, z_lo), gy: 16 (over x, z_hi, core).
Axes of the slice: x: 4, y: 8, z: 8 (z_hi: 2, z_lo: 4; z = z_hi * 4 + z_lo), core: 2. Of those that a mesh axis runs over, the one named last changes fastest.
Arguments:
- density: bfloat16 [32, 32, 8, 128, 128], P('gx', 'gy'), may hold values from -0.09375 to 0.09375
- intersection: bfloat16 [32, 32, 8, 128, 128], P('gx', 'gy'), may hold values from -6 to 6
- columns: int32 [32, 32, 8], P('gx', 'gy'), may hold values from 0 to 1023, as said below
- counts: int32 [32, 32], P('gx', 'gy'), may hold values from 4 to 8, as said below
Outputs:
- purified: float32 [32, 32, 8, 128, 128], P('gx', 'gy')
Inputs may be any that keep to these rules, and one draw needn't show every extreme that they name: `columns`: the first counts entries of a row are distinct block rows at most one step away from it in each grid direction, one of them the row itself; later entries are further such rows or the row itself. `counts`: rows at grid corners have 4, and the interior row (1, 1) has 8.
All inputs are finite; a program needn't handle non-finite values.
Results may differ from a plain program's by a relative error of at most 0.0049.
Values may be sent and summed in bfloat16 or wider, within the bound.
A program may use at most 64 MiB of HBM per device.

v0:
```python
import jax
import jax.numpy as jnp
from jax import lax
from jax.sharding import PartitionSpec as P


def with_halo(block, sides, width):
    for axis, dim in sides:
        count = lax.axis_size(axis)
        forward = [(i, i + 1) for i in range(count - 1)]
        backward = [(target, source) for source, target in forward]
        low = lax.ppermute(
            lax.slice_in_dim(block, block.shape[dim] - width, None, axis=dim), axis, forward
        )
        high = lax.ppermute(lax.slice_in_dim(block, 0, width, axis=dim), axis, backward)
        block = jnp.concatenate([low, block, high], axis=dim)
    return block


def on_device(density, intersection, columns, counts):
    rows_x, rows_y, slots_n = columns.shape
    block = density.shape[-1]
    rows = rows_x * rows_y
    slots = jnp.arange(slots_n, dtype=jnp.int32)
    pattern = jnp.where(slots[None, None, :] < counts[:, :, None], columns, -1)
    rim_pattern = with_halo(pattern, (("gx", 0), ("gy", 1)), 1)
    index_x = lax.axis_index("gx")
    index_y = lax.axis_index("gy")
    grid_y = rows_y * lax.axis_size("gy")
    live = pattern >= 0
    local_x = pattern // grid_y - index_x * rows_x + 1
    local_y = pattern % grid_y - index_y * rows_y + 1
    self_flat = (
        (jnp.arange(rows_x, dtype=jnp.int32)[:, None, None] + 1) * (rows_y + 2)
        + jnp.arange(rows_y, dtype=jnp.int32)[None, :, None]
        + 1
    )
    neighbor = jnp.where(live, local_x * (rows_y + 2) + local_y, self_flat + 0 * pattern).reshape(
        rows, slots_n
    )
    their = rim_pattern.reshape(-1, slots_n)[neighbor]
    pattern_rows = pattern.reshape(rows, slots_n)
    live_rows = live.reshape(rows, slots_n)
    match = (
        (their[:, :, :, None] == pattern_rows[:, None, None, :])
        & live_rows[:, None, None, :]
        & live_rows[:, :, None, None]
    )
    onehot = match.astype(jnp.bfloat16)

    def product(left, rim):
        gathered = rim.reshape(-1, slots_n, block, block)[neighbor]
        chosen = jnp.einsum(
            "rkbc,rkbxy->rkcxy", onehot, gathered, preferred_element_type=jnp.float32
        ).astype(jnp.bfloat16)
        result = jnp.einsum(
            "rkxy,rkcyz->rcxz",
            left.reshape(rows, slots_n, block, block),
            chosen,
            preferred_element_type=jnp.float32,
        )
        return result.reshape(rows_x, rows_y, slots_n, block, block)

    intersection_side = with_halo(intersection, (("gx", 0), ("gy", 1)), 1)
    lsprod = product(density, intersection_side).astype(jnp.bfloat16)
    density_side = with_halo(density, (("gx", 0), ("gy", 1)), 1)
    lslprod = product(lsprod, density_side).astype(jnp.bfloat16)
    cubic_side = with_halo(lslprod, (("gx", 0), ("gy", 1)), 1)
    quintic = product(lsprod, cubic_side)
    return 3.0 * lslprod.astype(jnp.float32) - 2.0 * quintic


def solution(mesh):
    placed = (
        P("gx", "gy", None, None, None),
        P("gx", "gy", None, None, None),
        P("gx", "gy", None),
        P("gx", "gy"),
    )
    return jax.shard_map(
        on_device,
        mesh=mesh,
        in_specs=placed,
        out_specs=P("gx", "gy", None, None, None),
        check_vma=False,
    )
```

profile of v0, /device:TPU:164, one launch (start us, length us, event | category | flops | bytes accessed | tf_op | source)
XLA Modules:
  0.0 278.0 jit_solution(17571582755745198237)
XLA Ops:
  0.0 0.8 fusion.58
  0.8 4.3 %collective-permute-start = (s32[1,2,8]{2,1,0:T(2,128)S(1)}, s32[1,2,8]{2,1,0:T(2,128)S(1)}, u32[]{:S(2)}, u32[]{:S(2)}) collective-permute-start(s32[1,2,8]{2,1,0:T(2,128)S(1)} %get-tuple-element.6), channel_id=1, source_target_pairs={{0,16},{16,32},{32,48},{48,64},{64,80},{80,96},{96,112},{112,128},... | collective-permute-start | bytes 200 | tf_op jit(solution)/shard_map/ppermute | solution.py:12
  5.0 1.9 collective-permute-start.1
  7.0 3.9 %collective-permute-start.8 = (bf16[1,2,8,128,128]{4,3,2,1,0:T(8,128)(2,1)}, bf16[1,2,8,128,128]{4,3,2,1,0:T(8,128)(2,1)S(1)}, u32[]{:S(2)}, u32[]{:S(2)}) collective-permute-start(bf16[1,2,8,128,128]{4,3,2,1,0:T(8,128)(2,1)} %param.5), channel_id=1, source_target_pairs={{0,16},{16,32},{32,48},{48,64},{64,80},{80,96},{96,112},{112,128},... | collective-permute-start | bytes 1572872 | tf_op jit(solution)/shard_map/ppermute | solution.py:12
  10.9 1.9 collective-permute-start.9
  12.8 4.6 %collective-permute-start.4 = (bf16[1,2,8,128,128]{4,3,2,1,0:T(8,128)(2,1)}, bf16[1,2,8,128,128]{4,3,2,1,0:T(8,128)(2,1)S(1)}, u32[]{:S(2)}, u32[]{:S(2)}) collective-permute-start(bf16[1,2,8,128,128]{4,3,2,1,0:T(8,128)(2,1)} %param.4), channel_id=1, source_target_pairs={{0,16},{16,32},{32,48},{48,64},{64,80},{80,96},{96,112},{112,128},... | collective-permute-start | bytes 1572872 | tf_op jit(solution)/shard_map/ppermute | solution.py:12
  17.6 1.9 collective-permute-start.5
  19.6 1.9 collective-permute-start.2
  21.5 24.9 %collective-permute-done.8 = bf16[1,2,8,128,128]{4,3,2,1,0:T(8,128)(2,1)S(1)} collective-permute-done((bf16[1,2,8,128,128]{4,3,2,1,0:T(8,128)(2,1)}, bf16[1,2,8,128,128]{4,3,2,1,0:T(8,128)(2,1)S(1)}, u32[]{:S(2)}, u32[]{:S(2)}) %collective-permute-start.8) | collective-permute-done | bytes 524320 | tf_op jit(solution)/shard_map/ppermute | solution.py:12
  46.4 5.0 %collective-permute-start.3 = (s32[3,1,8]{2,1,0:T(1,128)S(1)}, s32[3,1,8]{2,1,0:T(1,128)S(1)}, u32[]{:S(2)}, u32[]{:S(2)}) collective-permute-start(s32[3,1,8]{2,1,0:T(1,128)S(1)} %get-tuple-element.14), channel_id=1, source_target_pairs={{1,0},{2,1},{3,2},{4,3},{5,4},{6,5},{7,6},{8,7},{9,8},{10,9},{11,1... | collective-permute-start | bytes 296 | tf_op jit(solution)/shard_map/ppermute | solution.py:15
  51.4 1.2 constant_dynamic-update-slice_fusion.4
  52.7 1.2 copy-done
  54.0 1.9 collective-permute-start.10
  55.9 4.5 %collective-permute-done.2 = s32[3,1,8]{2,1,0:T(1,128)S(1)} collective-permute-done((s32[3,1,8]{2,1,0:T(1,128)S(1)}, s32[3,1,8]{2,1,0:T(1,128)S(1)}, u32[]{:S(2)}, u32[]{:S(2)}) %collective-permute-start.2) | collective-permute-done | bytes 128 | tf_op jit(solution)/shard_map/ppermute | solution.py:12
  60.4 3.9 %collective-permute-start.11 = (bf16[3,1,8,128,128]{4,3,2,1,0:T(8,128)(2,1)S(1)}, bf16[3,1,8,128,128]{4,3,2,1,0:T(8,128)(2,1)}, u32[]{:S(2)}, u32[]{:S(2)}) collective-permute-start(bf16[3,1,8,128,128]{4,3,2,1,0:T(8,128)(2,1)S(1)} %get-tuple-element.12), channel_id=1, source_target_pairs={{1,0},{2,1},{3,2},{4,3},{5,4},{6,5},{7,6},{8,7},{9,8},{10,9},{11,1... | collective-permute-start | bytes 2359304 | tf_op jit(solution)/shard_map/ppermute | solution.py:15
  64.4 0.6 gather_fusion
  65.2 1.2 constant_dynamic-update-slice_fusion
  66.4 1.6 fusion.60
  67.9 1.9 collective-permute-start.6
  69.9 8.4 %collective-permute-start.7 = (bf16[3,1,8,128,128]{4,3,2,1,0:T(8,128)(2,1)}, bf16[3,1,8,128,128]{4,3,2,1,0:T(8,128)(2,1)}, u32[]{:S(2)}, u32[]{:S(2)}) collective-permute-start(bf16[3,1,8,128,128]{4,3,2,1,0:T(8,128)(2,1)} %get-tuple-element.10), channel_id=1, source_target_pairs={{1,0},{2,1},{3,2},{4,3},{5,4},{6,5},{7,6},{8,7},{9,8},{10,9},{11,1... | collective-permute-start | bytes 2359304 | tf_op jit(solution)/shard_map/ppermute | solution.py:15
  78.3 2.6 collective-permute-done.10
  81.0 0.9 copy-done.10
  81.8 8.8 %collective-permute-done.11 = bf16[3,1,8,128,128]{4,3,2,1,0:T(8,128)(2,1)} collective-permute-done((bf16[3,1,8,128,128]{4,3,2,1,0:T(8,128)(2,1)S(1)}, bf16[3,1,8,128,128]{4,3,2,1,0:T(8,128)(2,1)}, u32[]{:S(2)}, u32[]{:S(2)}) %collective-permute-start.11) | collective-permute-done | bytes 786464 | tf_op jit(solution)/shard_map/ppermute | solution.py:15
  90.7 1.7 pad_maximum_fusion.1
  92.4 3.1 %gather_fusion.2 = bf16[16,8,128,128]{3,2,1,0:T(8,128)(2,1)} fusion(bf16[12,8,128,128]{3,2,1,0:T(8,128)(2,1)S(1)} %bitcast.79, s32[1024]{0:T(1024)S(1)} %pad_clamp_fusion), kind=kCustom, calls=%fused_computation.2 | custom fusion | bytes 8388672 | tf_op jit(solution)/shard_map/gather | solution.py:52
  95.5 6.6 %fusion = bf16[2,8,8,128,128]{4,2,3,1,0:T(8,128)(2,1)} fusion(bf16[2,8,8,128,128]{4,3,2,1,0:T(8,128)(2,1)} %bitcast.81, s32[2,8]{1,0:T(2,128)S(1)} %bitcast.91, s32[2,8,8]{2,1,0:T(8,128)S(1)} %bitcast.88, pred[2,8]{1,0:T(4,128)(4,1)S(1)} %get-tuple-element.5), kind=kOutput, calls=%fused_computation.4 | convolution fusion | flops 33557504 | bytes 8389200 | tf_op jit(solution)/shard_map/rkbc,rkbxy->rkcxy/dot_general | solution.py:53
  102.1 6.7 %copy.19 = bf16[2,8,8,128,128]{3,4,1,2,0:T(8,128)(2,1)} copy(bf16[2,8,8,128,128]{4,2,3,1,0:T(8,128)(2,1)} %fusion) | data formatting | bytes 8388608 | tf_op jit(solution)/shard_map/rkbc,rkbxy->rkcxy/dot_general | solution.py:53
  108.7 4.3 %fusion.37 = bf16[2,8,128,128,1]{2,3,1,4,0:T(8,128)(2,1)} fusion(bf16[2,8,8,128,128]{3,4,1,2,0:T(8,128)(2,1)} %copy.19, bf16[1,2,8,128,128]{4,3,2,1,0:T(8,128)(2,1)S(1)} %copy-done.9), kind=kOutput, calls=%fused_computation.27 | convolution fusion | flops 537133056 | bytes 5242880 | tf_op jit(solution)/shard_map/rkxy,rkcyz->rcxz/dot_general | solution.py:56
  113.1 1.7 pad_maximum_fusion
  114.8 3.1 %gather_fusion.1 = bf16[16,8,128,128]{3,2,1,0:T(8,128)(2,1)} fusion(bf16[12,8,128,128]{3,2,1,0:T(8,128)(2,1)S(1)} %bitcast.80, s32[1024]{0:T(1024)S(1)} %pad_clamp_fusion), kind=kCustom, calls=%fused_computation.1 | custom fusion | bytes 8388672 | tf_op jit(solution)/shard_map/gather | solution.py:52
  117.9 6.6 %fusion.2 = bf16[2,8,8,128,128]{4,2,3,1,0:T(8,128)(2,1)} fusion(bf16[2,8,8,128,128]{4,3,2,1,0:T(8,128)(2,1)} %bitcast.83, s32[2,8]{1,0:T(2,128)S(1)} %bitcast.92, s32[2,8,8]{2,1,0:T(8,128)S(1)} %bitcast.89, pred[2,8]{1,0:T(4,128)(4,1)S(1)} %get-tuple-element.5), kind=kOutput, calls=%fused_computation.6 | convolution fusion | flops 33557504 | bytes 8389200 | tf_op jit(solution)/shard_map/rkbc,rkbxy->rkcxy/dot_general | solution.py:53
  124.5 6.7 %copy.17 = bf16[2,8,8,128,128]{3,4,1,2,0:T(8,128)(2,1)} copy(bf16[2,8,8,128,128]{4,2,3,1,0:T(8,128)(2,1)} %fusion.2) | data formatting | bytes 8388608 | tf_op jit(solution)/shard_map/rkbc,rkbxy->rkcxy/dot_general | solution.py:53
  131.2 3.4 %fusion.34 = bf16[2,8,128,128]{3,2,1,0:T(8,128)(2,1)S(1)} fusion(bf16[2,8,128,128,1]{2,3,1,4,0:T(8,128)(2,1)S(1)} %copy-done.6, bf16[2,8,8,128,128]{3,4,1,2,0:T(8,128)(2,1)} %copy.17), kind=kOutput, calls=%fused_computation.26 | convolution fusion | flops 537133056 | bytes 5242880 | tf_op jit(solution)/shard_map/rkxy,rkcyz->rcxz/dot_general | solution.py:56
  134.6 1.9 collective-permute-start.12
  136.6 29.4 %collective-permute-start.13 = (bf16[1,2,8,128,128]{3,4,2,1,0:T(8,128)(2,1)S(1)}, bf16[1,2,8,128,128]{3,4,2,1,0:T(8,128)(2,1)S(1)}, u32[]{:S(2)}, u32[]{:S(2)}) collective-permute-start(bf16[1,2,8,128,128]{3,4,2,1,0:T(8,128)(2,1)S(1)} %bitcast.85), channel_id=1, source_target_pairs={{16,0},{32,16},{48,32},{64,48},{80,64},{96,80},{112,96},{128,112},... | collective-permute-start | bytes 1572872 | tf_op jit(solution)/shard_map/ppermute | solution.py:15
  166.0 21.7 %collective-permute-done.12 = bf16[1,2,8,128,128]{3,4,2,1,0:T(8,128)(2,1)S(1)} collective-permute-done((bf16[1,2,8,128,128]{3,4,2,1,0:T(8,128)(2,1)S(1)}, bf16[1,2,8,128,128]{3,4,2,1,0:T(8,128)(2,1)S(1)}, u32[]{:S(2)}, u32[]{:S(2)}) %collective-permute-start.12) | collective-permute-done | bytes 524320 | tf_op jit(solution)/shard_map/ppermute | solution.py:12
  187.7 25.9 %collective-permute-done.13 = bf16[1,2,8,128,128]{3,4,2,1,0:T(8,128)(2,1)S(1)} collective-permute-done((bf16[1,2,8,128,128]{3,4,2,1,0:T(8,128)(2,1)S(1)}, bf16[1,2,8,128,128]{3,4,2,1,0:T(8,128)(2,1)S(1)}, u32[]{:S(2)}, u32[]{:S(2)}) %collective-permute-start.13) | collective-permute-done | bytes 524320 | tf_op jit(solution)/shard_map/ppermute | solution.py:15
  213.6 0.2 pad_maximum_fusion.3
  213.9 2.1 collective-permute-start.14
  215.9 8.5 %collective-permute-start.15 = (bf16[3,1,8,128,128]{3,4,2,1,0:T(8,128)(2,1)S(1)}, bf16[3,1,8,128,128]{3,4,2,1,0:T(8,128)(2,1)S(1)}, u32[]{:S(2)}, u32[]{:S(2)}) collective-permute-start(bf16[3,1,8,128,128]{3,4,2,1,0:T(8,128)(2,1)S(1)} %get-tuple-element.8), channel_id=1, source_target_pairs={{1,0},{2,1},{3,2},{4,3},{5,4},{6,5},{7,6},{8,7},{9,8},{10,9},{11,1... | collective-permute-start | bytes 2359304 | tf_op jit(solution)/shard_map/ppermute | solution.py:15
  224.4 27.3 %collective-permute-done.14 = bf16[3,1,8,128,128]{3,4,2,1,0:T(8,128)(2,1)S(1)} collective-permute-done((bf16[3,1,8,128,128]{3,4,2,1,0:T(8,128)(2,1)S(1)}, bf16[3,1,8,128,128]{3,4,2,1,0:T(8,128)(2,1)S(1)}, u32[]{:S(2)}, u32[]{:S(2)}) %collective-permute-start.14) | collective-permute-done | bytes 786464 | tf_op jit(solution)/shard_map/ppermute | solution.py:12
  251.7 0.4 pad_maximum_fusion.2
  252.1 3.1 %gather_fusion.3 = bf16[16,8,128,128]{2,3,1,0:T(8,128)(2,1)} fusion(bf16[12,8,128,128]{2,3,1,0:T(8,128)(2,1)S(1)} %bitcast.78, s32[1024]{0:T(1024)S(1)} %pad_clamp_fusion), kind=kCustom, calls=%fused_computation.3 | custom fusion | bytes 8388672 | tf_op jit(solution)/shard_map/gather | solution.py:52
  255.2 6.5 %copy.24 = bf16[2,8,8,128,128]{4,2,3,1,0:T(8,128)(2,1)} copy(bf16[2,8,8,128,128]{3,4,2,1,0:T(8,128)(2,1)} %bitcast.82) | data formatting | bytes 8388608 | tf_op jit(solution)/shard_map/gather | solution.py:52
  261.7 4.9 %fusion.41 = bf16[2,8,8,128,128]{4,2,3,1,0:T(8,128)(2,1)} fusion(bf16[2,8,8,128,128]{4,2,3,1,0:T(8,128)(2,1)} %copy.24, s32[2,8]{1,0:T(2,128)S(1)} %bitcast.93, s32[2,8,8]{2,1,0:T(8,128)S(1)} %bitcast.90, pred[2,8]{1,0:T(4,128)(4,1)S(1)} %get-tuple-element.5), kind=kOutput, calls=%fused_computation.29 | convolution fusion | flops 33557504 | bytes 8389200 | tf_op jit(solution)/shard_map/rkbc,rkbxy->rkcxy/dot_general | solution.py:53
  266.6 6.7 %copy.25 = bf16[2,8,8,128,128]{3,4,1,2,0:T(8,128)(2,1)} copy(bf16[2,8,8,128,128]{4,2,3,1,0:T(8,128)(2,1)} %fusion.41) | data formatting | bytes 8388608 | tf_op jit(solution)/shard_map/rkbc,rkbxy->rkcxy/dot_general | solution.py:53
  273.3 3.4 %fusion.28 = f32[1,2,8,128,128]{3,4,2,1,0:T(8,128)S(1)} fusion(bf16[2,8,128,128,1]{2,3,1,4,0:T(8,128)(2,1)S(1)} %copy-done.7, bf16[2,8,8,128,128]{3,4,1,2,0:T(8,128)(2,1)} %copy.25, bf16[2,8,128,128]{3,2,1,0:T(8,128)(2,1)S(1)} %copy-done.5), kind=kOutput, calls=%fused_computation.24 | convolution fusion | flops 537919488 | bytes 6291456 | tf_op jit(solution)/shard_map/rkxy,rkcyz->rcxz/dot_general | solution.py:56
  276.7 1.3 copy.14
  (43 shorter events, 0.7 us)
Async XLA Ops:
  0.8 16.9 %collective-permute-start = (s32[1,2,8]{2,1,0:T(2,128)S(1)}, s32[1,2,8]{2,1,0:T(2,128)S(1)}, u32[]{:S(2)}, u32[]{:S(2)}) collective-permute-start(s32[1,2,8]{2,1,0:T(2,128)S(1)} %get-tuple-element.6), channel_id=1, source_target_pairs={{0,16},{16,32},{32,48},{48,64},{64,80},{80,96},{96,112},{112,128},... | collective-permute-start | bytes 200 | tf_op jit(solution)/shard_map/ppermute | solution.py:12
  5.0 14.5 %collective-permute-start.1 = (s32[1,2,8]{2,1,0:T(2,128)S(1)}, s32[1,2,8]{2,1,0:T(2,128)S(1)}, u32[]{:S(2)}, u32[]{:S(2)}) collective-permute-start(s32[1,2,8]{2,1,0:T(2,128)S(1)} %get-tuple-element.6), channel_id=1, source_target_pairs={{16,0},{32,16},{48,32},{64,48},{80,64},{96,80},{112,96},{128,112},... | collective-permute-start | bytes 200 | tf_op jit(solution)/shard_map/ppermute | solution.py:15
  7.0 39.4 %collective-permute-start.8 = (bf16[1,2,8,128,128]{4,3,2,1,0:T(8,128)(2,1)}, bf16[1,2,8,128,128]{4,3,2,1,0:T(8,128)(2,1)S(1)}, u32[]{:S(2)}, u32[]{:S(2)}) collective-permute-start(bf16[1,2,8,128,128]{4,3,2,1,0:T(8,128)(2,1)} %param.5), channel_id=1, source_target_pairs={{0,16},{16,32},{32,48},{48,64},{64,80},{80,96},{96,112},{112,128},... | collective-permute-start | bytes 1572872 | tf_op jit(solution)/shard_map/ppermute | solution.py:12
  10.9 41.7 %collective-permute-start.9 = (bf16[1,2,8,128,128]{4,3,2,1,0:T(8,128)(2,1)}, bf16[1,2,8,128,128]{4,3,2,1,0:T(8,128)(2,1)S(1)}, u32[]{:S(2)}, u32[]{:S(2)}) collective-permute-start(bf16[1,2,8,128,128]{4,3,2,1,0:T(8,128)(2,1)} %param.5), channel_id=1, source_target_pairs={{16,0},{32,16},{48,32},{64,48},{80,64},{96,80},{112,96},{128,112},... | collective-permute-start | bytes 1572872 | tf_op jit(solution)/shard_map/ppermute | solution.py:15
  12.8 52.2 %collective-permute-start.4 = (bf16[1,2,8,128,128]{4,3,2,1,0:T(8,128)(2,1)}, bf16[1,2,8,128,128]{4,3,2,1,0:T(8,128)(2,1)S(1)}, u32[]{:S(2)}, u32[]{:S(2)}) collective-permute-start(bf16[1,2,8,128,128]{4,3,2,1,0:T(8,128)(2,1)} %param.4), channel_id=1, source_target_pairs={{0,16},{16,32},{32,48},{48,64},{64,80},{80,96},{96,112},{112,128},... | collective-permute-start | bytes 1572872 | tf_op jit(solution)/shard_map/ppermute | solution.py:12
  17.6 47.5 %collective-permute-start.5 = (bf16[1,2,8,128,128]{4,3,2,1,0:T(8,128)(2,1)}, bf16[1,2,8,128,128]{4,3,2,1,0:T(8,128)(2,1)}, u32[]{:S(2)}, u32[]{:S(2)}) collective-permute-start(bf16[1,2,8,128,128]{4,3,2,1,0:T(8,128)(2,1)} %param.4), channel_id=1, source_target_pairs={{16,0},{32,16},{48,32},{64,48},{80,64},{96,80},{112,96},{128,112},... | collective-permute-start | bytes 1572872 | tf_op jit(solution)/shard_map/ppermute | solution.py:15
  19.6 40.8 %collective-permute-start.2 = (s32[3,1,8]{2,1,0:T(1,128)S(1)}, s32[3,1,8]{2,1,0:T(1,128)S(1)}, u32[]{:S(2)}, u32[]{:S(2)}) collective-permute-start(s32[3,1,8]{2,1,0:T(1,128)S(1)} %get-tuple-element.13), channel_id=1, source_target_pairs={{0,1},{1,2},{2,3},{3,4},{4,5},{5,6},{6,7},{7,8},{8,9},{9,10},{10,1... | collective-permute-start | bytes 296 | tf_op jit(solution)/shard_map/ppermute | solution.py:12
  46.4 18.0 %collective-permute-start.3 = (s32[3,1,8]{2,1,0:T(1,128)S(1)}, s32[3,1,8]{2,1,0:T(1,128)S(1)}, u32[]{:S(2)}, u32[]{:S(2)}) collective-permute-start(s32[3,1,8]{2,1,0:T(1,128)S(1)} %get-tuple-element.14), channel_id=1, source_target_pairs={{1,0},{2,1},{3,2},{4,3},{5,4},{6,5},{7,6},{8,7},{9,8},{10,9},{11,1... | collective-permute-start | bytes 296 | tf_op jit(solution)/shard_map/ppermute | solution.py:15
  51.4 13.7 %copy-start.8 = (bf16[1,2,8,128,128]{4,3,2,1,0:T(8,128)(2,1)S(1)}, bf16[1,2,8,128,128]{4,3,2,1,0:T(8,128)(2,1)}, u32[]{:S(2)}) copy-start(bf16[1,2,8,128,128]{4,3,2,1,0:T(8,128)(2,1)} %param.4) | copy-start | bytes 1572868
  52.7 1.2 copy-start
  54.0 27.0 %collective-permute-start.10 = (bf16[3,1,8,128,128]{4,3,2,1,0:T(8,128)(2,1)S(1)}, bf16[3,1,8,128,128]{4,3,2,1,0:T(8,128)(2,1)S(1)}, u32[]{:S(2)}, u32[]{:S(2)}) collective-permute-start(bf16[3,1,8,128,128]{4,3,2,1,0:T(8,128)(2,1)S(1)} %get-tuple-element.11), channel_id=1, source_target_pairs={{0,1},{1,2},{2,3},{3,4},{4,5},{5,6},{6,7},{7,8},{8,9},{9,10},{10,1... | collective-permute-start | bytes 2359304 | tf_op jit(solution)/shard_map/ppermute | solution.py:12
  60.4 30.2 %collective-permute-start.11 = (bf16[3,1,8,128,128]{4,3,2,1,0:T(8,128)(2,1)S(1)}, bf16[3,1,8,128,128]{4,3,2,1,0:T(8,128)(2,1)}, u32[]{:S(2)}, u32[]{:S(2)}) collective-permute-start(bf16[3,1,8,128,128]{4,3,2,1,0:T(8,128)(2,1)S(1)} %get-tuple-element.12), channel_id=1, source_target_pairs={{1,0},{2,1},{3,2},{4,3},{5,4},{6,5},{7,6},{8,7},{9,8},{10,9},{11,1... | collective-permute-start | bytes 2359304 | tf_op jit(solution)/shard_map/ppermute | solution.py:15
  65.0 25.7 %copy-start.1 = (bf16[3,2,8,128,128]{4,3,2,1,0:T(8,128)(2,1)S(1)}, bf16[3,2,8,128,128]{4,3,2,1,0:T(8,128)(2,1)}, u32[]{:S(2)}) copy-start(bf16[3,2,8,128,128]{4,3,2,1,0:T(8,128)(2,1)} %copy-done) | copy-start | bytes 4718596
  66.4 14.6 %copy-start.2 = (bf16[3,2,8,128,128]{4,3,2,1,0:T(8,128)(2,1)}, bf16[3,2,8,128,128]{4,3,2,1,0:T(8,128)(2,1)S(1)}, u32[]{:S(2)}) copy-start(bf16[3,2,8,128,128]{4,3,2,1,0:T(8,128)(2,1)S(1)} %constant_dynamic-update-slice_fusion) | copy-start | bytes 4718596
  67.9 45.2 %collective-permute-start.6 = (bf16[3,1,8,128,128]{4,3,2,1,0:T(8,128)(2,1)}, bf16[3,1,8,128,128]{4,3,2,1,0:T(8,128)(2,1)}, u32[]{:S(2)}, u32[]{:S(2)}) collective-permute-start(bf16[3,1,8,128,128]{4,3,2,1,0:T(8,128)(2,1)} %get-tuple-element.9), channel_id=1, source_target_pairs={{0,1},{1,2},{2,3},{3,4},{4,5},{5,6},{6,7},{7,8},{8,9},{9,10},{10,1... | collective-permute-start | bytes 2359304 | tf_op jit(solution)/shard_map/ppermute | solution.py:12
  69.9 43.2 %collective-permute-start.7 = (bf16[3,1,8,128,128]{4,3,2,1,0:T(8,128)(2,1)}, bf16[3,1,8,128,128]{4,3,2,1,0:T(8,128)(2,1)}, u32[]{:S(2)}, u32[]{:S(2)}) collective-permute-start(bf16[3,1,8,128,128]{4,3,2,1,0:T(8,128)(2,1)} %get-tuple-element.10), channel_id=1, source_target_pairs={{1,0},{2,1},{3,2},{4,3},{5,4},{6,5},{7,6},{8,7},{9,8},{10,9},{11,1... | collective-permute-start | bytes 2359304 | tf_op jit(solution)/shard_map/ppermute | solution.py:15
  81.0 0.9 copy-start.10
  102.1 6.7 %copy-start.9 = (bf16[1,2,8,128,128]{4,3,2,1,0:T(8,128)(2,1)S(1)}, bf16[1,2,8,128,128]{4,3,2,1,0:T(8,128)(2,1)}, u32[]{:S(2)}) copy-start(bf16[1,2,8,128,128]{4,3,2,1,0:T(8,128)(2,1)} %param.4) | copy-start | bytes 1572868
  108.7 4.4 %copy-start.3 = (bf16[3,2,8,128,128]{4,3,2,1,0:T(8,128)(2,1)S(1)}, bf16[3,2,8,128,128]{4,3,2,1,0:T(8,128)(2,1)}, u32[]{:S(2)}) copy-start(bf16[3,2,8,128,128]{4,3,2,1,0:T(8,128)(2,1)} %copy-done.2) | copy-start | bytes 4718596
  124.5 6.7 %copy-start.6 = (bf16[2,8,128,128,1]{2,3,1,4,0:T(8,128)(2,1)S(1)}, bf16[2,8,128,128,1]{2,3,1,4,0:T(8,128)(2,1)}, u32[]{:S(2)}) copy-start(bf16[2,8,128,128,1]{2,3,1,4,0:T(8,128)(2,1)} %fusion.37) | copy-start | bytes 1572868
  134.6 117.1 %copy-start.4 = (bf16[2,8,128,128]{3,2,1,0:T(8,128)(2,1)}, bf16[2,8,128,128]{3,2,1,0:T(8,128)(2,1)S(1)}, u32[]{:S(2)}) copy-start(bf16[2,8,128,128]{3,2,1,0:T(8,128)(2,1)S(1)} %fusion.34) | copy-start | bytes 1572868
  134.6 53.1 %collective-permute-start.12 = (bf16[1,2,8,128,128]{3,4,2,1,0:T(8,128)(2,1)S(1)}, bf16[1,2,8,128,128]{3,4,2,1,0:T(8,128)(2,1)S(1)}, u32[]{:S(2)}, u32[]{:S(2)}) collective-permute-start(bf16[1,2,8,128,128]{3,4,2,1,0:T(8,128)(2,1)S(1)} %bitcast.84), channel_id=1, source_target_pairs={{0,16},{16,32},{32,48},{48,64},{64,80},{80,96},{96,112},{112,128},... | collective-permute-start | bytes 1572872 | tf_op jit(solution)/shard_map/ppermute | solution.py:12
  136.6 77.0 %collective-permute-start.13 = (bf16[1,2,8,128,128]{3,4,2,1,0:T(8,128)(2,1)S(1)}, bf16[1,2,8,128,128]{3,4,2,1,0:T(8,128)(2,1)S(1)}, u32[]{:S(2)}, u32[]{:S(2)}) collective-permute-start(bf16[1,2,8,128,128]{3,4,2,1,0:T(8,128)(2,1)S(1)} %bitcast.85), channel_id=1, source_target_pairs={{16,0},{32,16},{48,32},{64,48},{80,64},{96,80},{112,96},{128,112},... | collective-permute-start | bytes 1572872 | tf_op jit(solution)/shard_map/ppermute | solution.py:15
  213.9 37.8 %collective-permute-start.14 = (bf16[3,1,8,128,128]{3,4,2,1,0:T(8,128)(2,1)S(1)}, bf16[3,1,8,128,128]{3,4,2,1,0:T(8,128)(2,1)S(1)}, u32[]{:S(2)}, u32[]{:S(2)}) collective-permute-start(bf16[3,1,8,128,128]{3,4,2,1,0:T(8,128)(2,1)S(1)} %get-tuple-element.7), channel_id=1, source_target_pairs={{0,1},{1,2},{2,3},{3,4},{4,5},{5,6},{6,7},{7,8},{8,9},{9,10},{10,1... | collective-permute-start | bytes 2359304 | tf_op jit(solution)/shard_map/ppermute | solution.py:12
  215.9 35.7 %collective-permute-start.15 = (bf16[3,1,8,128,128]{3,4,2,1,0:T(8,128)(2,1)S(1)}, bf16[3,1,8,128,128]{3,4,2,1,0:T(8,128)(2,1)S(1)}, u32[]{:S(2)}, u32[]{:S(2)}) collective-permute-start(bf16[3,1,8,128,128]{3,4,2,1,0:T(8,128)(2,1)S(1)} %get-tuple-element.8), channel_id=1, source_target_pairs={{1,0},{2,1},{3,2},{4,3},{5,4},{6,5},{7,6},{8,7},{9,8},{10,9},{11,1... | collective-permute-start | bytes 2359304 | tf_op jit(solution)/shard_map/ppermute | solution.py:15
  266.6 6.7 %copy-start.5 = (bf16[2,8,128,128]{3,2,1,0:T(8,128)(2,1)S(1)}, bf16[2,8,128,128]{3,2,1,0:T(8,128)(2,1)}, u32[]{:S(2)}) copy-start(bf16[2,8,128,128]{3,2,1,0:T(8,128)(2,1)} %copy-done.4) | copy-start | bytes 1572868
  266.6 6.7 %copy-start.7 = (bf16[2,8,128,128,1]{2,3,1,4,0:T(8,128)(2,1)S(1)}, bf16[2,8,128,128,1]{2,3,1,4,0:T(8,128)(2,1)}, u32[]{:S(2)}) copy-start(bf16[2,8,128,128,1]{2,3,1,4,0:T(8,128)(2,1)} %fusion.37) | copy-start | bytes 1572868
where the time goes:
time: 279 us; the launch traced here: 278 us
  waiting for transfers between devices  116 us (42%)
  starting transfers between devices  83.5 us (30%)
  local copies, waits for them, and re-layouts  44.2 us (16%)
  matrix products  29.2 us (10%)
  other arithmetic  4.93 us (2%)
    ppermute x8, waiting for transfers between devices, with_halo(): lax.ppermute(lax.slice_in_dim(block, block.shape[dim] - width, None, axis...  81 us
    ppermute x8, starting transfers between devices, with_halo(): lax.ppermute(lax.slice_in_dim(block, 0, width, axis=dim), axis, backward)  61 us
    ppermute x8, waiting for transfers between devices, with_halo(): lax.ppermute(lax.slice_in_dim(block, 0, width, axis=dim), axis, backward)  34.7 us
    ppermute x8, starting transfers between devices, with_halo(): lax.ppermute(lax.slice_in_dim(block, block.shape[dim] - width, None, axis...  22.6 us
    dot_general x3, local copies, waits for them, and re-layouts, product(): jnp.einsum('rkbc,rkbxy->rkcxy', onehot, gathered, preferred_element_type=...  20 us
    dot_general x3, matrix products, product(): jnp.einsum('rkbc,rkbxy->rkcxy', onehot, gathered, preferred_element_type=...  18 us
    gather x4, local copies, waits for them, and re-layouts, product(): gathered = rim.reshape(-1, slots_n, block, block)[neighbor]  15.8 us
    dot_general x3, matrix products, product(): jnp.einsum('rkxy,rkcyz->rcxz', left.reshape(rows, slots_n, block, block),...  11.2 us
  transfers between devices with their start and end apart: 16, of which 7 were waited for; matrix products, arithmetic and copies ran while one was open for 10% of the time, Pallas kernels for 0%

commit v1 on v0

v1 whole, which is shorter than its diff:
```python
import functools

import jax
import jax.numpy as jnp
from jax import lax
from jax.experimental import pallas as pl
from jax.experimental.pallas import tpu as pltpu
from jax.sharding import PartitionSpec as P

MESH = pl.DeviceIdType.MESH
BF16 = jnp.bfloat16
F32 = jnp.float32
STEPS = (-1, 0, 1)


def kernel(
    size_x, size_y, slots, l_hbm, s_hbm, cols, cnts, k_out,
    offs_out, offs, raw_s, raw_l, bs, bl, bq, ls, kst, kret,
    t_send, t_recv, o_send, o_recv, h_send, h_recv, k_send, k_recv,
):
    gx = lax.axis_index("gx")
    gy = lax.axis_index("gy")
    y, r = gx // 4, gx % 4
    x, h, k = gy // 4, (gy // 2) % 2, gy % 2
    z = 4 * h + r

    def dev(x_, y_, z_, k_):
        return (y_ * 4 + z_ % 4, (x_ * 2 + z_ // 4) * 2 + k_)

    keeps = r // 2 == k
    at_slot = r % 2
    to = [dev(x, y, 4 * h + 2 * k + j, r // 2) for j in range(2)]
    home = [dev(x, y, 4 * h + 2 * k + q, r // 2) for q in range(2)]
    home_row = r % 2
    stays = [jnp.logical_and(keeps, at_slot == j) for j in range(2)]

    up_z = z + 1
    z_next = dev((x + up_z // 8) % size_x, y, up_z % 8, k)
    dn_z = z + 7
    z_prev = dev((x + size_x - 1 + dn_z // 8) % size_x, y, dn_z % 8, k)
    x_next = dev(x, (y + k) % size_y, z, 1 - k)
    x_prev = dev(x, (y + size_y - 1 + k) % size_y, z, 1 - k)

    barrier = pltpu.get_barrier_semaphore()
    for d in (z_next, z_prev, x_next, x_prev):
        pl.semaphore_signal(barrier, inc=1, device_id=d, device_id_type=MESH)
    for j in range(2):
        @pl.when(jnp.logical_not(stays[j]))
        def _():
            pl.semaphore_signal(barrier, inc=1, device_id=to[j], device_id_type=MESH)
            pl.semaphore_signal(barrier, inc=1, device_id=home[j], device_id_type=MESH)

    grid_y = 8 * size_x
    for j in range(2):
        for b in range(slots):
            col = cols[0, j, b]
            dx = col // grid_y - gx
            dy = col % grid_y - (2 * gy + j)
            offs_out[j, b] = jnp.where(b < cnts[0, j], (dy + 1) * 3 + dx + 1, 9)

    zero = jnp.zeros((128, 128), BF16)
    for q in range(2):
        raw_s[q, slots] = zero
        raw_l[q, slots] = zero
        kst[q, 9] = zero

    pl.semaphore_wait(barrier, jnp.where(keeps, 6, 8))

    def send(src, dst, j, ssem, rsem, d):
        return pltpu.make_async_remote_copy(
            src_ref=src, dst_ref=dst, send_sem=ssem, recv_sem=rsem,
            device_id=d, device_id_type=MESH,
        )

    def arrive(dst, sem):
        pltpu.make_async_copy(dst, dst, sem).wait()

    live = pl.ds(0, slots)
    outs = []

    def route(src, dst, ssem, rsem, j, d):
        cp = send(src, dst, j, ssem, rsem, d)

        @pl.when(jnp.logical_not(stays[j]))
        def _():
            cp.start()

        @pl.when(stays[j])
        def _():
            pltpu.make_async_copy(src, dst, rsem).start()

        outs.append((cp, j))

    for j in range(2):
        route(offs_out.at[j], offs.at[at_slot], o_send.at[j], o_recv.at[at_slot], j, to[j])
    for m, (src, raw) in enumerate(((s_hbm, raw_s), (l_hbm, raw_l))):
        for j in range(2):
            route(
                src.at[0, j], raw.at[at_slot, live],
                t_send.at[m, j], t_recv.at[m, at_slot], j, to[j],
            )

    for q in range(2):
        arrive(offs.at[q], o_recv.at[q])
    place = []
    for q in range(2):
        mine = [offs[q, b] for b in range(slots)]
        row = []
        for d in range(9):
            s = jnp.int32(slots)
            for b in range(slots):
                s = jnp.where(mine[b] == d, b, s)
            row.append(s)
        place.append(row)

    def spread(m, raw, out):
        for q in range(2):
            arrive(raw.at[q, live], t_recv.at[m, q])
        for q in range(2):
            for d in range(9):
                out[1 + q, 1, d // 3, d % 3] = raw[q, place[q][d]]

    def side(m, b):
        c = []
        for n, (src, dst, d) in enumerate((
            (b.at[pl.ds(1, 2), 1, pl.ds(1, 2)], b.at[pl.ds(1, 2), 0, pl.ds(1, 2)], z_next),
            (b.at[pl.ds(1, 2), 1, pl.ds(0, 2)], b.at[pl.ds(1, 2), 2, pl.ds(0, 2)], z_prev),
            (b.at[2, 1, :, pl.ds(1, 2)], b.at[0, 1, :, pl.ds(1, 2)], x_next),
            (b.at[1, 1, :, pl.ds(0, 2)], b.at[3, 1, :, pl.ds(0, 2)], x_prev),
        )):
            cp = send(src, dst, 0, h_send.at[m, n], h_recv.at[m, n], d)
            cp.start()
            c.append(cp)
        return c

    def corners(m, b, c):
        c[0].wait_recv()
        c[1].wait_recv()
        n = 4
        for ny, dys in ((0, pl.ds(1, 2)), (2, pl.ds(0, 2))):
            for src, dst, dxs, d in ((2, 0, pl.ds(1, 2), x_next), (1, 3, pl.ds(0, 2), x_prev)):
                cp = send(
                    b.at[src, ny, dys, dxs], b.at[dst, ny, dys, dxs],
                    0, h_send.at[m, n], h_recv.at[m, n], d,
                )
                cp.start()
                c.append(cp)
                n += 1

    def joined(c):
        for cp in c[2:]:
            cp.wait_recv()

    def cell(a, b, q, cy, cx):
        near = [
            (ny, nx) for ny in STEPS for nx in STEPS
            if abs(cy - ny) <= 1 and abs(cx - nx) <= 1
        ]
        lhs = jnp.concatenate([a(q, ny, nx) for ny, nx in near], axis=1)
        rhs = jnp.concatenate(
            [b[1 + q + nx, 1 + ny, cy - ny + 1, cx - nx + 1] for ny, nx in near], axis=0
        )
        return jnp.dot(lhs, rhs, preferred_element_type=F32)

    def trunc(value, q, d):
        return jnp.where(place[q][d] < slots, value, 0.0).astype(BF16)

    spread(0, raw_s, bs)
    c_s = side(0, bs)
    spread(1, raw_l, bl)
    c_l = side(1, bl)
    corners(0, bs, c_s)
    joined(c_s)

    def left_l(q, ny, nx):
        return bl[1 + q, 1, ny + 1, nx + 1]

    def left_ls(q, ny, nx):
        return ls[q, (ny + 1) * 3 + nx + 1]

    for q in range(2):
        for cy in STEPS:
            for cx in STEPS:
                d = (cy + 1) * 3 + cx + 1
                ls[q, d] = trunc(cell(left_l, bs, q, cy, cx), q, d)
    corners(1, bl, c_l)
    joined(c_l)
    for q in range(2):
        for cy in STEPS:
            for cx in STEPS:
                d = (cy + 1) * 3 + cx + 1
                bq[1 + q, 1, cy + 1, cx + 1] = trunc(cell(left_ls, bl, q, cy, cx), q, d)
    c_q = side(2, bq)
    corners(2, bq, c_q)
    joined(c_q)
    backs = []
    for q in range(2):
        for cy in STEPS:
            for cx in STEPS:
                d = (cy + 1) * 3 + cx + 1
                lsl = bq[1 + q, 1, cy + 1, cx + 1].astype(F32)
                kst[q, d] = (3.0 * lsl - 2.0 * cell(left_ls, bq, q, cy, cx)).astype(BF16)
        for b in range(slots):
            kret[q, b] = kst[q, offs[q, b]]
        cp = send(
            kret.at[q], k_out.at[0, home_row], 0, k_send.at[q], k_recv.at[home_row], home[q]
        )

        @pl.when(jnp.logical_not(stays[q]))
        def _():
            cp.start()

        @pl.when(stays[q])
        def _():
            pltpu.make_async_copy(kret.at[q], k_out.at[0, home_row], k_recv.at[home_row]).start()

        outs.append((cp, q))

    for c in (c_s, c_l, c_q):
        for cp in c:
            cp.wait_send()
    for cp, j in outs:
        @pl.when(jnp.logical_not(stays[j]))
        def _():
            cp.wait_send()
    for j in range(2):
        arrive(k_out.at[0, j], k_recv.at[j])


def on_device(density, intersection, columns, counts):
    size_y = lax.axis_size("gx") // 4
    size_x = lax.axis_size("gy") // 4
    slots = columns.shape[-1]
    block = (128, 128)
    dma = pltpu.SemaphoreType.DMA
    purified = pl.pallas_call(
        functools.partial(kernel, size_x, size_y, slots),
        out_shape=jax.ShapeDtypeStruct(density.shape, BF16),
        in_specs=[
            pl.BlockSpec(memory_space=pl.ANY),
            pl.BlockSpec(memory_space=pl.ANY),
            pl.BlockSpec(memory_space=pltpu.SMEM),
            pl.BlockSpec(memory_space=pltpu.SMEM),
        ],
        out_specs=pl.BlockSpec(memory_space=pl.ANY),
        scratch_shapes=[
            pltpu.SMEM((2, slots), jnp.int32),
            pltpu.SMEM((2, slots), jnp.int32),
            pltpu.VMEM((2, slots + 1) + block, BF16),
            pltpu.VMEM((2, slots + 1) + block, BF16),
            pltpu.VMEM((4, 3, 3, 3) + block, BF16),
            pltpu.VMEM((4, 3, 3, 3) + block, BF16),
            pltpu.VMEM((4, 3, 3, 3) + block, BF16),
            pltpu.VMEM((2, 9) + block, BF16),
            pltpu.VMEM((2, 10) + block, BF16),
            pltpu.VMEM((2, slots) + block, BF16),
            dma((2, 2)), dma((2, 2)),
            dma((2,)), dma((2,)),
            dma((3, 8)), dma((3, 8)),
            dma((2,)), dma((2,)),
        ],
        compiler_params=pltpu.CompilerParams(
            collective_id=0, has_side_effects=True, vmem_limit_bytes=40 << 20
        ),
        cost_estimate=pl.CostEstimate(
            flops=3 * 2 * 49 * 2 * 128**3, bytes_accessed=3 << 20, transcendentals=0
        ),
    )(density, intersection, columns, counts)
    return purified.astype(F32)


def solution(mesh):
    placed = (
        P("gx", "gy", None, None, None),
        P("gx", "gy", None, None, None),
        P("gx", "gy", None),
        P("gx", "gy"),
    )
    return jax.shard_map(
        on_device,
        mesh=mesh,
        in_specs=placed,
        out_specs=P("gx", "gy", None, None, None),
        check_vma=False,
    )
```

time: 279 us -> 91.3 us (0.33)
  the two profiles are of different devices: /device:TPU:164 before, /device:TPU:1 now
where the time goes in v1:
time: 91.3 us; the launch traced here: 90.9 us
  Pallas kernels  86.4 us (95%)
  local copies, waits for them, and re-layouts  3.42 us (4%)
  other arithmetic  1.07 us (1%)
    pallas_call x1, Pallas kernels, on_device(): pl.pallas_call(functools.partial(kernel, size_x, size_y, slots), out_shap...  86.4 us
    unnamed x8, local copies, waits for them, and re-layouts  3.42 us

profile of v1, /device:TPU:1, one launch (start us, length us, event | category | flops | bytes accessed | tf_op | source)
XLA Modules:
  0.0 90.9 jit_solution(1654918532276630669)
XLA Ops:
  0.0 0.0 copy-start
  0.0 1.0 %copy-done = bf16[1,2,8,128,128]{4,3,2,1,0:T(8,128)(2,1)S(1)} copy-done((bf16[1,2,8,128,128]{4,3,2,1,0:T(8,128)(2,1)S(1)}, bf16[1,2,8,128,128]{4,3,2,1,0:T(8,128)(2,1)}, u32[]{:S(2)}) %copy-start) | copy-done | bytes 524312
  1.0 0.0 copy-start.1
  1.0 1.0 %copy-done.1 = bf16[1,2,8,128,128]{4,3,2,1,0:T(8,128)(2,1)S(1)} copy-done((bf16[1,2,8,128,128]{4,3,2,1,0:T(8,128)(2,1)S(1)}, bf16[1,2,8,128,128]{4,3,2,1,0:T(8,128)(2,1)}, u32[]{:S(2)}) %copy-start.1) | copy-done | bytes 524312
  2.1 0.0 copy-start.2
  2.1 0.7 copy-done.2
  2.8 0.0 copy-start.3
  2.8 0.7 copy-done.3
  3.4 86.4 %shard_map.46 = bf16[1,2,8,128,128]{4,3,2,1,0:T(8,128)(2,1)S(1)} custom-call(bf16[1,2,8,128,128]{4,3,2,1,0:T(8,128)(2,1)S(1)} %copy-done, bf16[1,2,8,128,128]{4,3,2,1,0:T(8,128)(2,1)S(1)} %copy-done.1, s32[1,2,8]{2,1,0:T(2,128)S(1)} %copy-done.2, s32[1,2]{1,0:T(1,128)S(1)} %copy-done.3), custom_call_target="tpu_custom_call" | custom-call | flops 1233125376 | bytes 3145728 | tf_op jit(solution)/shard_map/pallas_call | solution.py:236
  89.8 1.1 %convert_element_type.3 = f32[1,2,8,128,128]{4,3,2,1,0:T(8,128)} convert(bf16[1,2,8,128,128]{4,3,2,1,0:T(8,128)(2,1)S(1)} %shard_map.46) | non-fusion elementwise | flops 262144 | bytes 1572864 | tf_op jit(solution)/shard_map/convert_element_type | solution.py:269
Async XLA Ops:
  0.0 1.0 %copy-start = (bf16[1,2,8,128,128]{4,3,2,1,0:T(8,128)(2,1)S(1)}, bf16[1,2,8,128,128]{4,3,2,1,0:T(8,128)(2,1)}, u32[]{:S(2)}) copy-start(bf16[1,2,8,128,128]{4,3,2,1,0:T(8,128)(2,1)} %l_hbm.1) | copy-start | bytes 1572868
  1.0 1.0 %copy-start.1 = (bf16[1,2,8,128,128]{4,3,2,1,0:T(8,128)(2,1)S(1)}, bf16[1,2,8,128,128]{4,3,2,1,0:T(8,128)(2,1)}, u32[]{:S(2)}) copy-start(bf16[1,2,8,128,128]{4,3,2,1,0:T(8,128)(2,1)} %s_hbm.1) | copy-start | bytes 1572868
  2.1 0.7 copy-start.2
  2.8 0.7 copy-start.3

commit v2 on v1

--- a/solution.py
+++ b/solution.py
@@ -14,8 +14,8 @@
 
 
 def kernel(
-    size_x, size_y, slots, l_hbm, s_hbm, cols, cnts, k_out,
-    offs_out, offs, raw_s, raw_l, bs, bl, bq, ls, kst, kret,
+    size_x, size_y, slots, l_hbm, s_hbm, cols_hbm, cnts_hbm, k_out,
+    cols, cnts, arg_sem, offs_out, offs, raw_s, raw_l, bs, bl, bq, ls, kst, kret,
     t_send, t_recv, o_send, o_recv, h_send, h_recv, k_send, k_recv,
 ):
     gx = lax.axis_index("gx")
@@ -38,11 +38,18 @@
     z_next = dev((x + up_z // 8) % size_x, y, up_z % 8, k)
     dn_z = z + 7
     z_prev = dev((x + size_x - 1 + dn_z // 8) % size_x, y, dn_z % 8, k)
-    x_next = dev(x, (y + k) % size_y, z, 1 - k)
-    x_prev = dev(x, (y + size_y - 1 + k) % size_y, z, 1 - k)
-
+    y_peer = dev(x, (y + size_y - 1 + 2 * k) % size_y, z, 1 - k)
+    sibling = dev(x, y, z, 1 - k)
+    q_out, q_in = k, 1 - k
+
+    pattern_in = [
+        pltpu.make_async_copy(cols_hbm, cols, arg_sem.at[0]),
+        pltpu.make_async_copy(cnts_hbm, cnts, arg_sem.at[1]),
+    ]
+    for cp in pattern_in:
+        cp.start()
     barrier = pltpu.get_barrier_semaphore()
-    for d in (z_next, z_prev, x_next, x_prev):
+    for d in (z_next, z_prev, y_peer, sibling):
         pl.semaphore_signal(barrier, inc=1, device_id=d, device_id_type=MESH)
     for j in range(2):
         @pl.when(jnp.logical_not(stays[j]))
@@ -50,6 +57,8 @@
             pl.semaphore_signal(barrier, inc=1, device_id=to[j], device_id_type=MESH)
             pl.semaphore_signal(barrier, inc=1, device_id=home[j], device_id_type=MESH)
 
+    for cp in pattern_in:
+        cp.wait()
     grid_y = 8 * size_x
     for j in range(2):
         for b in range(slots):
@@ -89,7 +98,7 @@
         def _():
             pltpu.make_async_copy(src, dst, rsem).start()
 
-        outs.append((cp, j))
+        outs.append((cp, stays[j]))
 
     for j in range(2):
         route(offs_out.at[j], offs.at[at_slot], o_send.at[j], o_recv.at[at_slot], j, to[j])
@@ -120,32 +129,44 @@
             for d in range(9):
                 out[1 + q, 1, d // 3, d % 3] = raw[q, place[q][d]]
 
-    def side(m, b):
-        c = []
-        for n, (src, dst, d) in enumerate((
-            (b.at[pl.ds(1, 2), 1, pl.ds(1, 2)], b.at[pl.ds(1, 2), 0, pl.ds(1, 2)], z_next),
-            (b.at[pl.ds(1, 2), 1, pl.ds(0, 2)], b.at[pl.ds(1, 2), 2, pl.ds(0, 2)], z_prev),
-            (b.at[2, 1, :, pl.ds(1, 2)], b.at[0, 1, :, pl.ds(1, 2)], x_next),
-            (b.at[1, 1, :, pl.ds(0, 2)], b.at[3, 1, :, pl.ds(0, 2)], x_prev),
-        )):
-            cp = send(src, dst, 0, h_send.at[m, n], h_recv.at[m, n], d)
-            cp.start()
-            c.append(cp)
-        return c
-
-    def corners(m, b, c):
-        c[0].wait_recv()
-        c[1].wait_recv()
-        n = 4
-        for ny, dys in ((0, pl.ds(1, 2)), (2, pl.ds(0, 2))):
-            for src, dst, dxs, d in ((2, 0, pl.ds(1, 2), x_next), (1, 3, pl.ds(0, 2), x_prev)):
-                cp = send(
-                    b.at[src, ny, dys, dxs], b.at[dst, ny, dys, dxs],
-                    0, h_send.at[m, n], h_recv.at[m, n], d,
-                )
-                cp.start()
-                c.append(cp)
-                n += 1
+    def halo(m, b, n, src, dst, d):
+        cp = send(src, dst, 0, h_send.at[m, n], h_recv.at[m, n], d)
+        cp.start()
+        return cp
+
+    def side_out(m, b):
+        nx = 1 + q_out
+        return [
+            halo(m, b, 0, b.at[nx, 1, pl.ds(1, 2)], b.at[nx, 0, pl.ds(1, 2)], z_next),
+            halo(m, b, 1, b.at[nx, 1, pl.ds(0, 2)], b.at[nx, 2, pl.ds(0, 2)], z_prev),
+            halo(m, b, 2, b.at[nx, 1, :, pl.ds(k, 2)], b.at[3 - 3 * k, 1, :, pl.ds(k, 2)], y_peer),
+        ]
+
+    def side_in(m, b):
+        nx = 1 + q_in
+        return [
+            halo(m, b, 5, b.at[nx, 1, pl.ds(1, 2)], b.at[nx, 0, pl.ds(1, 2)], z_next),
+            halo(m, b, 6, b.at[nx, 1, pl.ds(0, 2)], b.at[nx, 2, pl.ds(0, 2)], z_prev),
+            halo(m, b, 7, b.at[nx, 1, :, pl.ds(1 - k, 2)], b.at[3 * k, 1, :, pl.ds(1 - k, 2)], sibling),
+        ]
+
+    def corners_out(m, b, c):
+        nx = 1 + q_out
+        for n, (ny, dy) in enumerate(((0, 1), (2, 0))):
+            c[n].wait_recv()
+            c.append(halo(
+                m, b, 3 + n, b.at[nx, ny, pl.ds(dy, 2), pl.ds(k, 2)],
+                b.at[3 - 3 * k, ny, pl.ds(dy, 2), pl.ds(k, 2)], y_peer,
+            ))
+
+    def corners_in(m, b, c):
+        nx = 1 + q_in
+        for n, (ny, dy) in enumerate(((0, 1), (2, 0))):
+            c[n].wait_recv()
+            c.append(halo(
+                m, b, 8 + n, b.at[nx, ny, pl.ds(dy, 2), pl.ds(1 - k, 2)],
+                b.at[3 * k, ny, pl.ds(dy, 2), pl.ds(1 - k, 2)], sibling,
+            ))
 
     def joined(c):
         for cp in c[2:]:
@@ -162,15 +183,15 @@
         )
         return jnp.dot(lhs, rhs, preferred_element_type=F32)
 
-    def trunc(value, q, d):
-        return jnp.where(place[q][d] < slots, value, 0.0).astype(BF16)
-
     spread(0, raw_s, bs)
-    c_s = side(0, bs)
+    c_s_out, c_s_in = side_out(0, bs), side_in(0, bs)
     spread(1, raw_l, bl)
-    c_l = side(1, bl)
-    corners(0, bs, c_s)
-    joined(c_s)
+    c_l_out, c_l_in = side_out(1, bl), side_in(1, bl)
+    corners_out(0, bs, c_s_out)
+    corners_in(0, bs, c_s_in)
+    joined(c_s_out)
+    joined(c_s_in)
+    corners_out(1, bl, c_l_out)
 
     def left_l(q, ny, nx):
         return bl[1 + q, 1, ny + 1, nx + 1]
@@ -178,49 +199,61 @@
     def left_ls(q, ny, nx):
         return ls[q, (ny + 1) * 3 + nx + 1]
 
-    for q in range(2):
-        for cy in STEPS:
-            for cx in STEPS:
-                d = (cy + 1) * 3 + cx + 1
-                ls[q, d] = trunc(cell(left_l, bs, q, cy, cx), q, d)
-    corners(1, bl, c_l)
-    joined(c_l)
-    for q in range(2):
-        for cy in STEPS:
-            for cx in STEPS:
-                d = (cy + 1) * 3 + cx + 1
-                bq[1 + q, 1, cy + 1, cx + 1] = trunc(cell(left_ls, bl, q, cy, cx), q, d)
-    c_q = side(2, bq)
-    corners(2, bq, c_q)
-    joined(c_q)
-    backs = []
-    for q in range(2):
-        for cy in STEPS:
-            for cx in STEPS:
-                d = (cy + 1) * 3 + cx + 1
-                lsl = bq[1 + q, 1, cy + 1, cx + 1].astype(F32)
-                kst[q, d] = (3.0 * lsl - 2.0 * cell(left_ls, bq, q, cy, cx)).astype(BF16)
+    def product(q, left, right, out):
+        for d in range(9):
+            dy, dx = d // 3, d % 3
+            used = jnp.where(q == 0, place[0][d], place[1][d]) < slots
+            value = cell(left, right, q, dy - 1, dx - 1)
+            out(q, dy, dx, jnp.where(used, value, 0.0).astype(BF16))
+
+    def put_ls(q, dy, dx, value):
+        ls[q, dy * 3 + dx] = value
+
+    def put_lsl(q, dy, dx, value):
+        bq[1 + q, 1, dy, dx] = value
+
+    product(q_out, left_l, bs, put_ls)
+    product(q_in, left_l, bs, put_ls)
+    corners_in(1, bl, c_l_in)
+    joined(c_l_out)
+    joined(c_l_in)
+    product(q_out, left_ls, bl, put_lsl)
+    c_q_out = side_out(2, bq)
+    product(q_in, left_ls, bl, put_lsl)
+    c_q_in = side_in(2, bq)
+    corners_out(2, bq, c_q_out)
+    corners_in(2, bq, c_q_in)
+    joined(c_q_in)
+    for n, q in enumerate((q_in, q_out)):
+        if n == 1:
+            joined(c_q_out)
+        for d in range(9):
+            dy, dx = d // 3, d % 3
+            lsl = bq[1 + q, 1, dy, dx].astype(F32)
+            kst[q, d] = (3.0 * lsl - 2.0 * cell(left_ls, bq, q, dy - 1, dx - 1)).astype(BF16)
         for b in range(slots):
             kret[q, b] = kst[q, offs[q, b]]
+        there = dev(x, y, 4 * h + 2 * k + q, r // 2)
+        stay = jnp.logical_and(keeps, at_slot == q)
         cp = send(
-            kret.at[q], k_out.at[0, home_row], 0, k_send.at[q], k_recv.at[home_row], home[q]
+            kret.at[q], k_out.at[0, home_row], 0, k_send.at[n], k_recv.at[home_row], there
         )
 
-        @pl.when(jnp.logical_not(stays[q]))
+        @pl.when(jnp.logical_not(stay))
         def _():
             cp.start()
 
-        @pl.when(stays[q])
+        @pl.when(stay)
         def _():
             pltpu.make_async_copy(kret.at[q], k_out.at[0, home_row], k_recv.at[home_row]).start()
 
-        outs.append((cp, q))
-
-    for c in (c_s, c_l, c_q):
+        outs.append((cp, stay))
+
+    for c in (c_s_out, c_s_in, c_l_out, c_l_in, c_q_out, c_q_in):
         for cp in c:
             cp.wait_send()
-    for cp, j in outs:
-        @pl.when(jnp.logical_not(stays[j]))
+    for cp, stay in outs:
+        @pl.when(jnp.logical_not(stay))
         def _():
             cp.wait_send()
     for j in range(2):
@@ -239,11 +272,14 @@
         in_specs=[
             pl.BlockSpec(memory_space=pl.ANY),
             pl.BlockSpec(memory_space=pl.ANY),
-            pl.BlockSpec(memory_space=pltpu.SMEM),
-            pl.BlockSpec(memory_space=pltpu.SMEM),
+            pl.BlockSpec(memory_space=pl.ANY),
+            pl.BlockSpec(memory_space=pl.ANY),
         ],
         out_specs=pl.BlockSpec(memory_space=pl.ANY),
         scratch_shapes=[
+            pltpu.SMEM(columns.shape, jnp.int32),
+            pltpu.SMEM(counts.shape, jnp.int32),
+            dma((2,)),
             pltpu.SMEM((2, slots), jnp.int32),
             pltpu.SMEM((2, slots), jnp.int32),
             pltpu.VMEM((2, slots + 1) + block, BF16),
@@ -256,11 +292,11 @@
             pltpu.VMEM((2, slots) + block, BF16),
             dma((2, 2)), dma((2, 2)),
             dma((2,)), dma((2,)),
-            dma((3, 8)), dma((3, 8)),
+            dma((3, 10)), dma((3, 10)),
             dma((2,)), dma((2,)),
         ],
         compiler_params=pltpu.CompilerParams(
-            collective_id=0, has_side_effects=True, vmem_limit_bytes=40 << 20
+            collective_id=0, has_side_effects=True, vmem_limit_bytes=60 << 20
         ),
         cost_estimate=pl.CostEstimate(
             flops=3 * 2 * 49 * 2 * 128**3, bytes_accessed=3 << 20, transcendentals=0

time: 91.3 us -> 81.6 us (0.89)
  Pallas kernels: 86.4 us -> 79.2 us
  local copies, waits for them, and re-layouts: 3.42 us -> 0 us
  other arithmetic: 1.07 us -> 2.12 us
    pallas_call x1, Pallas kernels: 86.4 us -> 79.2 us  [on_device(): pl.pallas_call(functools.partial(kernel, size_x, size_y, slots), out_shap...]
    unnamed x8 -> x0, local copies, waits for them, and re-layouts: 3.42 us -> none
    convert_element_type x1, other arithmetic: 1.07 us -> 2.12 us  [on_device(): return purified.astype(F32)]
where the time goes in v2:
time: 81.6 us; the launch traced here: 81.3 us
  Pallas kernels  79.2 us (97%)
  other arithmetic  2.12 us (3%)
    pallas_call x1, Pallas kernels, on_device(): pl.pallas_call(functools.partial(kernel, size_x, size_y, slots), out_shap...  79.2 us
    convert_element_type x1, other arithmetic, on_device(): return purified.astype(F32)  2.12 us

profile of v2, /device:TPU:1, one launch (start us, length us, event | category | flops | bytes accessed | tf_op | source)
XLA Modules:
  0.0 81.3 jit_solution(11422336196346579361)
XLA Ops:
  0.0 79.2 %shard_map.46 = bf16[1,2,8,128,128]{4,3,2,1,0:T(8,128)(2,1)} custom-call(bf16[1,2,8,128,128]{4,3,2,1,0:T(8,128)(2,1)} %l_hbm.1, bf16[1,2,8,128,128]{4,3,2,1,0:T(8,128)(2,1)} %s_hbm.1, s32[1,2,8]{2,1,0:T(2,128)} %cols_hbm.1, s32[1,2]{1,0:T(1,128)} %cnts_hbm.1), custom_call_target="tpu_custom_call" | custom-call | flops 1233125376 | bytes 3145728 | tf_op jit(solution)/shard_map/pallas_call | solution.py:269
  79.2 2.1 %convert_element_type.3 = f32[1,2,8,128,128]{4,3,2,1,0:T(8,128)} convert(bf16[1,2,8,128,128]{4,3,2,1,0:T(8,128)(2,1)} %shard_map.46) | non-fusion elementwise | flops 262144 | bytes 1572864 | tf_op jit(solution)/shard_map/convert_element_type | solution.py:305

commit v3 on v2

--- a/solution.py
+++ b/solution.py
@@ -41,6 +41,9 @@
     y_peer = dev(x, (y + size_y - 1 + 2 * k) % size_y, z, 1 - k)
     sibling = dev(x, y, z, 1 - k)
     q_out, q_in = k, 1 - k
+    has_next = jnp.logical_or(x < size_x - 1, z < 7)
+    has_prev = jnp.logical_or(x > 0, z > 0)
+    has_y = jnp.where(k == 0, y > 0, y < size_y - 1)
 
     pattern_in = [
         pltpu.make_async_copy(cols_hbm, cols, arg_sem.at[0]),
@@ -49,8 +52,12 @@
     for cp in pattern_in:
         cp.start()
     barrier = pltpu.get_barrier_semaphore()
-    for d in (z_next, z_prev, y_peer, sibling):
-        pl.semaphore_signal(barrier, inc=1, device_id=d, device_id_type=MESH)
+    pl.semaphore_signal(barrier, inc=1, device_id=sibling, device_id_type=MESH)
+    for there, d in ((has_next, z_next), (has_prev, z_prev), (has_y, y_peer)):
+        @pl.when(there)
+        def _():
+            pl.semaphore_signal(barrier, inc=1, device_id=d, device_id_type=MESH)
+
     for j in range(2):
         @pl.when(jnp.logical_not(stays[j]))
         def _():
@@ -68,12 +75,40 @@
             offs_out[j, b] = jnp.where(b < cnts[0, j], (dy + 1) * 3 + dx + 1, 9)
 
     zero = jnp.zeros((128, 128), BF16)
+
+    def blank(b, nx, ny):
+        def cell_row(i, _):
+            b[nx, ny, i // 3, i % 3] = zero
+            return 0
+
+        lax.fori_loop(0, 9, cell_row, 0)
+
+    for b in (bs, bl, bq):
+        @pl.when(jnp.logical_not(has_prev))
+        def _():
+            blank(b, 1, 0)
+            blank(b, 2, 0)
+
+        @pl.when(jnp.logical_not(has_next))
+        def _():
+            blank(b, 1, 2)
+            blank(b, 2, 2)
+
+        @pl.when(jnp.logical_not(has_y))
+        def _():
+            for ny in range(3):
+                blank(b, 3 * k, ny)
+
     for q in range(2):
         raw_s[q, slots] = zero
         raw_l[q, slots] = zero
         kst[q, 9] = zero
 
-    pl.semaphore_wait(barrier, jnp.where(keeps, 6, 8))
+    pl.semaphore_wait(
+        barrier,
+        jnp.where(keeps, 3, 5) + jnp.where(has_next, 1, 0) + jnp.where(has_prev, 1, 0)
+        + jnp.where(has_y, 1, 0),
+    )
 
     def send(src, dst, j, ssem, rsem, d):
         return pltpu.make_async_remote_copy(
@@ -103,11 +138,25 @@
     for j in range(2):
         route(offs_out.at[j], offs.at[at_slot], o_send.at[j], o_recv.at[at_slot], j, to[j])
     for m, (src, raw) in enumerate(((s_hbm, raw_s), (l_hbm, raw_l))):
-        for j in range(2):
-            route(
-                src.at[0, j], raw.at[at_slot, live],
-                t_send.at[m, j], t_recv.at[m, at_slot], j, to[j],
+        for j in (k, 1 - k):
+            stay = jnp.logical_and(keeps, at_slot == j)
+            there = dev(x, y, 4 * h + 2 * k + j, r // 2)
+            cp = send(
+                src.at[0, j], raw.at[at_slot, live], 0,
+                t_send.at[m, j], t_recv.at[m, at_slot], there,
             )
+
+            @pl.when(jnp.logical_not(stay))
+            def _():
+                cp.start()
+
+            @pl.when(stay)
+            def _():
+                pltpu.make_async_copy(
+                    src.at[0, j], raw.at[at_slot, live], t_recv.at[m, at_slot]
+                ).start()
+
+            outs.append((cp, stay))
 
     for q in range(2):
         arrive(offs.at[q], o_recv.at[q])
@@ -129,40 +178,66 @@
             for d in range(9):
                 out[1 + q, 1, d // 3, d % 3] = raw[q, place[q][d]]
 
-    def halo(m, b, n, src, dst, d):
+    def halo(m, b, n, src, dst, d, sent=None, comes=None):
         cp = send(src, dst, 0, h_send.at[m, n], h_recv.at[m, n], d)
-        cp.start()
-        return cp
+        if sent is None:
+            cp.start()
+        else:
+            pl.when(sent)(cp.start)
+        return cp, sent, comes
+
+    def landed(c):
+        cp, _, comes = c
+        if comes is None:
+            cp.wait_recv()
+        else:
+            pl.when(comes)(cp.wait_recv)
+
+    def left(c):
+        cp, sent, _ = c
+        if sent is None:
+            cp.wait_send()
+        else:
+            pl.when(sent)(cp.wait_send)
+
+    def along_z(m, b, n, q):
+        nx = 1 + q
+        return [
+            halo(
+                m, b, n, b.at[nx, 1, pl.ds(1, 2)], b.at[nx, 0, pl.ds(1, 2)],
+                z_next, has_next, has_prev,
+            ),
+            halo(
+                m, b, n + 1, b.at[nx, 1, pl.ds(0, 2)], b.at[nx, 2, pl.ds(0, 2)],
+                z_prev, has_prev, has_next,
+            ),
+        ]
 
     def side_out(m, b):
-        nx = 1 + q_out
-        return [
-            halo(m, b, 0, b.at[nx, 1, pl.ds(1, 2)], b.at[nx, 0, pl.ds(1, 2)], z_next),
-            halo(m, b, 1, b.at[nx, 1, pl.ds(0, 2)], b.at[nx, 2, pl.ds(0, 2)], z_prev),
-            halo(m, b, 2, b.at[nx, 1, :, pl.ds(k, 2)], b.at[3 - 3 * k, 1, :, pl.ds(k, 2)], y_peer),
-        ]
+        return along_z(m, b, 0, q_out) + [halo(
+            m, b, 2, b.at[1 + q_out, 1, :, pl.ds(k, 2)],
+            b.at[3 - 3 * k, 1, :, pl.ds(k, 2)], y_peer, has_y, has_y,
+        )]
 
     def side_in(m, b):
-        nx = 1 + q_in
-        return [
-            halo(m, b, 5, b.at[nx, 1, pl.ds(1, 2)], b.at[nx, 0, pl.ds(1, 2)], z_next),
-            halo(m, b, 6, b.at[nx, 1, pl.ds(0, 2)], b.at[nx, 2, pl.ds(0, 2)], z_prev),
-            halo(m, b, 7, b.at[nx, 1, :, pl.ds(1 - k, 2)], b.at[3 * k, 1, :, pl.ds(1 - k, 2)], sibling),
-        ]
+        return along_z(m, b, 5, q_in) + [halo(
+            m, b, 7, b.at[1 + q_in, 1, :, pl.ds(1 - k, 2)],
+            b.at[3 * k, 1, :, pl.ds(1 - k, 2)], sibling,
+        )]
 
     def corners_out(m, b, c):
         nx = 1 + q_out
         for n, (ny, dy) in enumerate(((0, 1), (2, 0))):
-            c[n].wait_recv()
+            landed(c[n])
             c.append(halo(
                 m, b, 3 + n, b.at[nx, ny, pl.ds(dy, 2), pl.ds(k, 2)],
-                b.at[3 - 3 * k, ny, pl.ds(dy, 2), pl.ds(k, 2)], y_peer,
+                b.at[3 - 3 * k, ny, pl.ds(dy, 2), pl.ds(k, 2)], y_peer, has_y, has_y,
             ))
 
     def corners_in(m, b, c):
         nx = 1 + q_in
         for n, (ny, dy) in enumerate(((0, 1), (2, 0))):
-            c[n].wait_recv()
+            landed(c[n])
             c.append(halo(
                 m, b, 8 + n, b.at[nx, ny, pl.ds(dy, 2), pl.ds(1 - k, 2)],
                 b.at[3 * k, ny, pl.ds(dy, 2), pl.ds(1 - k, 2)], sibling,
@@ -170,7 +245,7 @@
 
     def joined(c):
         for cp in c[2:]:
-            cp.wait_recv()
+            landed(cp)
 
     def cell(a, b, q, cy, cx):
         near = [
@@ -215,14 +290,14 @@
     product(q_out, left_l, bs, put_ls)
     product(q_in, left_l, bs, put_ls)
     corners_in(1, bl, c_l_in)
+    joined(c_l_in)
+    product(q_in, left_ls, bl, put_lsl)
+    c_q_in = side_in(2, bq)
     joined(c_l_out)
-    joined(c_l_in)
     product(q_out, left_ls, bl, put_lsl)
     c_q_out = side_out(2, bq)
-    product(q_in, left_ls, bl, put_lsl)
-    c_q_in = side_in(2, bq)
+    corners_in(2, bq, c_q_in)
     corners_out(2, bq, c_q_out)
-    corners_in(2, bq, c_q_in)
     joined(c_q_in)
     for n, q in enumerate((q_in, q_out)):
         if n == 1:
@@ -251,7 +326,7 @@
 
     for c in (c_s_out, c_s_in, c_l_out, c_l_in, c_q_out, c_q_in):
         for cp in c:
-            cp.wait_send()
+            left(cp)
     for cp, stay in outs:
         @pl.when(jnp.logical_not(stay))
         def _():

time: 81.6 us -> 78.3 us (0.960)
  Pallas kernels: 79.2 us -> 75.5 us
    pallas_call x1, Pallas kernels: 79.2 us -> 75.5 us  [on_device(): pl.pallas_call(functools.partial(kernel, size_x, size_y, slots), out_shap...]
where the time goes in v3:
time: 78.3 us; the launch traced here: 77.6 us
  Pallas kernels  75.5 us (96%)
  other arithmetic  2.12 us (3%)
    pallas_call x1, Pallas kernels, on_device(): pl.pallas_call(functools.partial(kernel, size_x, size_y, slots), out_shap...  75.5 us
    convert_element_type x1, other arithmetic, on_device(): return purified.astype(F32)  2.12 us

profile of v3, /device:TPU:1, one launch (start us, length us, event | category | flops | bytes accessed | tf_op | source)
XLA Modules:
  0.0 77.6 jit_solution(13747309446806396)
XLA Ops:
  0.0 75.5 %shard_map.46 = bf16[1,2,8,128,128]{4,3,2,1,0:T(8,128)(2,1)} custom-call(bf16[1,2,8,128,128]{4,3,2,1,0:T(8,128)(2,1)} %l_hbm.1, bf16[1,2,8,128,128]{4,3,2,1,0:T(8,128)(2,1)} %s_hbm.1, s32[1,2,8]{2,1,0:T(2,128)} %cols_hbm.1, s32[1,2]{1,0:T(1,128)} %cnts_hbm.1), custom_call_target="tpu_custom_call" | custom-call | flops 1233125376 | bytes 3145728 | tf_op jit(solution)/shard_map/pallas_call | solution.py:344
  75.5 2.1 %convert_element_type.3 = f32[1,2,8,128,128]{4,3,2,1,0:T(8,128)} convert(bf16[1,2,8,128,128]{4,3,2,1,0:T(8,128)(2,1)} %shard_map.46) | non-fusion elementwise | flops 262144 | bytes 1572864 | tf_op jit(solution)/shard_map/convert_element_type | solution.py:380

commit v4 on v3

--- a/solution.py
+++ b/solution.py
@@ -137,7 +137,7 @@
 
     for j in range(2):
         route(offs_out.at[j], offs.at[at_slot], o_send.at[j], o_recv.at[at_slot], j, to[j])
-    for m, (src, raw) in enumerate(((s_hbm, raw_s), (l_hbm, raw_l))):
+    def transpose(m, src, raw, when):
         for j in (k, 1 - k):
             stay = jnp.logical_and(keeps, at_slot == j)
             there = dev(x, y, 4 * h + 2 * k + j, r // 2)
@@ -146,20 +146,28 @@
                 t_send.at[m, j], t_recv.at[m, at_slot], there,
             )
 
-            @pl.when(jnp.logical_not(stay))
+            @pl.when(jnp.logical_and(when, jnp.logical_not(stay)))
             def _():
                 cp.start()
 
-            @pl.when(stay)
+            @pl.when(jnp.logical_and(when, stay))
             def _():
                 pltpu.make_async_copy(
                     src.at[0, j], raw.at[at_slot, live], t_recv.at[m, at_slot]
                 ).start()
 
-            outs.append((cp, stay))
-
+            if when is light:
+                outs.append((cp, stay))
+
+    light = keeps
+    heavy = jnp.logical_not(keeps)
+    transpose(0, s_hbm, raw_s, heavy)
+    transpose(1, l_hbm, raw_l, heavy)
     for q in range(2):
         arrive(offs.at[q], o_recv.at[q])
+    transpose(0, s_hbm, raw_s, light)
+    transpose(1, l_hbm, raw_l, light)
+
     place = []
     for q in range(2):
         mine = [offs[q, b] for b in range(slots)]
@@ -262,12 +270,6 @@
     c_s_out, c_s_in = side_out(0, bs), side_in(0, bs)
     spread(1, raw_l, bl)
     c_l_out, c_l_in = side_out(1, bl), side_in(1, bl)
-    corners_out(0, bs, c_s_out)
-    corners_in(0, bs, c_s_in)
-    joined(c_s_out)
-    joined(c_s_in)
-    corners_out(1, bl, c_l_out)
-
     def left_l(q, ny, nx):
         return bl[1 + q, 1, ny + 1, nx + 1]
 
@@ -287,12 +289,17 @@
     def put_lsl(q, dy, dx, value):
         bq[1 + q, 1, dy, dx] = value
 
-    product(q_out, left_l, bs, put_ls)
+    corners_out(0, bs, c_s_out)
+    corners_in(0, bs, c_s_in)
+    joined(c_s_in)
     product(q_in, left_l, bs, put_ls)
     corners_in(1, bl, c_l_in)
+    corners_out(1, bl, c_l_out)
     joined(c_l_in)
     product(q_in, left_ls, bl, put_lsl)
     c_q_in = side_in(2, bq)
+    joined(c_s_out)
+    product(q_out, left_l, bs, put_ls)
     joined(c_l_out)
     product(q_out, left_ls, bl, put_lsl)
     c_q_out = side_out(2, bq)

time: 78.3 us -> 77.1 us (0.985)
  no operation moved by 1% of the time
where the time goes in v4:
time: 77.1 us; the launch traced here: 76.9 us
  Pallas kernels  74.8 us (97%)
  other arithmetic  2.12 us (3%)
    pallas_call x1, Pallas kernels, on_device(): pl.pallas_call(functools.partial(kernel, size_x, size_y, slots), out_shap...  74.8 us
    convert_element_type x1, other arithmetic, on_device(): return purified.astype(F32)  2.12 us

profile of v4, /device:TPU:1, one launch (start us, length us, event | category | flops | bytes accessed | tf_op | source)
XLA Modules:
  0.0 76.9 jit_solution(16218567519276281965)
XLA Ops:
  0.0 74.8 %shard_map.46 = bf16[1,2,8,128,128]{4,3,2,1,0:T(8,128)(2,1)} custom-call(bf16[1,2,8,128,128]{4,3,2,1,0:T(8,128)(2,1)} %l_hbm.1, bf16[1,2,8,128,128]{4,3,2,1,0:T(8,128)(2,1)} %s_hbm.1, s32[1,2,8]{2,1,0:T(2,128)} %cols_hbm.1, s32[1,2]{1,0:T(1,128)} %cnts_hbm.1), custom_call_target="tpu_custom_call" | custom-call | flops 1233125376 | bytes 3145728 | tf_op jit(solution)/shard_map/pallas_call | solution.py:351
  74.8 2.1 %convert_element_type.3 = f32[1,2,8,128,128]{4,3,2,1,0:T(8,128)} convert(bf16[1,2,8,128,128]{4,3,2,1,0:T(8,128)(2,1)} %shard_map.46) | non-fusion elementwise | flops 262144 | bytes 1572864 | tf_op jit(solution)/shard_map/convert_element_type | solution.py:387

commit v5 on v4

--- a/solution.py
+++ b/solution.py
@@ -269,18 +269,33 @@
     spread(0, raw_s, bs)
     c_s_out, c_s_in = side_out(0, bs), side_in(0, bs)
     spread(1, raw_l, bl)
-    c_l_out, c_l_in = side_out(1, bl), side_in(1, bl)
+    c_l_in, c_l_out = side_in(1, bl), side_out(1, bl)
     def left_l(q, ny, nx):
         return bl[1 + q, 1, ny + 1, nx + 1]
 
     def left_ls(q, ny, nx):
         return ls[q, (ny + 1) * 3 + nx + 1]
+
+    def cells(a, b, q, cy):
+        near = [(ny, nx) for ny in STEPS for nx in STEPS if abs(cy - ny) <= 1]
+        lhs = jnp.concatenate([a(q, ny, nx) for ny, nx in near], axis=1)
+        rhs = jnp.concatenate([
+            jnp.concatenate([
+                b[1 + q + nx, 1 + ny, cy - ny + 1, cx - nx + 1] if cx - nx >= -1 else zero
+                for cx in (-1, 0)
+            ], axis=1)
+            for ny, nx in near
+        ], axis=0)
+        both = jnp.dot(lhs, rhs, preferred_element_type=F32)
+        return both[:, :128], both[:, 128:], cell(a, b, q, cy, 1)
 
     def product(q, left, right, out):
         for d in range(9):
             dy, dx = d // 3, d % 3
+            if dx == 0:
+                three = cells(left, right, q, dy - 1)
             used = jnp.where(q == 0, place[0][d], place[1][d]) < slots
-            value = cell(left, right, q, dy - 1, dx - 1)
+            value = three[dx]
             out(q, dy, dx, jnp.where(used, value, 0.0).astype(BF16))
 
     def put_ls(q, dy, dx, value):
@@ -311,8 +326,10 @@
             joined(c_q_out)
         for d in range(9):
             dy, dx = d // 3, d % 3
+            if dx == 0:
+                three = cells(left_ls, bq, q, dy - 1)
             lsl = bq[1 + q, 1, dy, dx].astype(F32)
-            kst[q, d] = (3.0 * lsl - 2.0 * cell(left_ls, bq, q, dy - 1, dx - 1)).astype(BF16)
+            kst[q, d] = (3.0 * lsl - 2.0 * three[dx]).astype(BF16)
         for b in range(slots):
             kret[q, b] = kst[q, offs[q, b]]
         there = dev(x, y, 4 * h + 2 * k + q, r // 2)

time: 77.1 us -> 75.9 us (0.984)
  Pallas kernels: 74.8 us -> 73.1 us
    pallas_call x1, Pallas kernels: 74.8 us -> 73.1 us  [on_device(): pl.pallas_call(functools.partial(kernel, size_x, size_y, slots), out_shap...]
where the time goes in v5:
time: 75.9 us; the launch traced here: 75.2 us
  Pallas kernels  73.1 us (96%)
  other arithmetic  2.12 us (3%)
    pallas_call x1, Pallas kernels, on_device(): pl.pallas_call(functools.partial(kernel, size_x, size_y, slots), out_shap...  73.1 us
    convert_element_type x1, other arithmetic, on_device(): return purified.astype(F32)  2.12 us

profile of v5, /device:TPU:1, one launch (start us, length us, event | category | flops | bytes accessed | tf_op | source)
XLA Modules:
  0.0 75.2 jit_solution(7404041988833875289)
XLA Ops:
  0.0 73.1 %shard_map.46 = bf16[1,2,8,128,128]{4,3,2,1,0:T(8,128)(2,1)} custom-call(bf16[1,2,8,128,128]{4,3,2,1,0:T(8,128)(2,1)} %l_hbm.1, bf16[1,2,8,128,128]{4,3,2,1,0:T(8,128)(2,1)} %s_hbm.1, s32[1,2,8]{2,1,0:T(2,128)} %cols_hbm.1, s32[1,2]{1,0:T(1,128)} %cnts_hbm.1), custom_call_target="tpu_custom_call" | custom-call | flops 1233125376 | bytes 3145728 | tf_op jit(solution)/shard_map/pallas_call | solution.py:368
  73.1 2.1 %convert_element_type.3 = f32[1,2,8,128,128]{4,3,2,1,0:T(8,128)} convert(bf16[1,2,8,128,128]{4,3,2,1,0:T(8,128)(2,1)} %shard_map.46) | non-fusion elementwise | flops 262144 | bytes 1572864 | tf_op jit(solution)/shard_map/convert_element_type | solution.py:404

commit v6 on v5

--- a/solution.py
+++ b/solution.py
@@ -267,7 +267,7 @@
         return jnp.dot(lhs, rhs, preferred_element_type=F32)
 
     spread(0, raw_s, bs)
-    c_s_out, c_s_in = side_out(0, bs), side_in(0, bs)
+    c_s_in, c_s_out = side_in(0, bs), side_out(0, bs)
     spread(1, raw_l, bl)
     c_l_in, c_l_out = side_in(1, bl), side_out(1, bl)
     def left_l(q, ny, nx):
@@ -304,8 +304,8 @@
     def put_lsl(q, dy, dx, value):
         bq[1 + q, 1, dy, dx] = value
 
+    corners_in(0, bs, c_s_in)
     corners_out(0, bs, c_s_out)
-    corners_in(0, bs, c_s_in)
     joined(c_s_in)
     product(q_in, left_l, bs, put_ls)
     corners_in(1, bl, c_l_in)

time: 75.9 us -> 75.9 us (level)
  no operation moved by 1% of the time
where the time goes in v6:
time: 75.9 us; the launch traced here: 75.2 us
  Pallas kernels  73.1 us (96%)
  other arithmetic  2.12 us (3%)
    pallas_call x1, Pallas kernels, on_device(): pl.pallas_call(functools.partial(kernel, size_x, size_y, slots), out_shap...  73.1 us
    convert_element_type x1, other arithmetic, on_device(): return purified.astype(F32)  2.12 us

profile of v6, /device:TPU:1, one launch (start us, length us, event | category | flops | bytes accessed | tf_op | source)
XLA Modules:
  0.0 75.2 jit_solution(3535528381284005614)
XLA Ops:
  0.0 73.1 %shard_map.46 = bf16[1,2,8,128,128]{4,3,2,1,0:T(8,128)(2,1)} custom-call(bf16[1,2,8,128,128]{4,3,2,1,0:T(8,128)(2,1)} %l_hbm.1, bf16[1,2,8,128,128]{4,3,2,1,0:T(8,128)(2,1)} %s_hbm.1, s32[1,2,8]{2,1,0:T(2,128)} %cols_hbm.1, s32[1,2]{1,0:T(1,128)} %cnts_hbm.1), custom_call_target="tpu_custom_call" | custom-call | flops 1233125376 | bytes 3145728 | tf_op jit(solution)/shard_map/pallas_call | solution.py:368
  73.1 2.1 %convert_element_type.3 = f32[1,2,8,128,128]{4,3,2,1,0:T(8,128)} convert(bf16[1,2,8,128,128]{4,3,2,1,0:T(8,128)(2,1)} %shard_map.46) | non-fusion elementwise | flops 262144 | bytes 1572864 | tf_op jit(solution)/shard_map/convert_element_type | solution.py:404
